TPU v7x, 32 devices: a whole 2x2x4 slice. The times are simulated.
32 devices in a mesh: px: 4 (over z), py: 8 (over y, x, core).
Axes of the slice: x: 2, y: 2, z: 4, core: 2. Of those that a mesh axis runs over, the one named last changes fastest.
Arguments:
- coupling: bfloat16 [4, 8, 64, 218, 125], P('px', 'py'), may hold values from -0.5 to 0.5
- interior_inverse: bfloat16 [4, 8, 64, 125, 125], P('px', 'py'), may hold values from -0.5 to 0.5
- interior_load: bfloat16 [4, 8, 64, 125, 256], P('px', 'py'), may hold values from -6 to 6
- boundary_load: bfloat16 [4, 8, 4608, 256], P('px', 'py'), may hold values from -6 to 6
- owner_weight: float32 [4, 8, 4608], P('px', 'py'), may hold values from 0.5 to 4
- elem_weight: float32 [4, 8, 64, 218], P('px', 'py'), may hold values from 0.25 to 1
- elem_dof: int32 [4, 8, 64, 218], P('px', 'py'), may hold values from 0 to 5999, as said below
- reader_rows: int32 [4, 8, 4, 348], P('px', 'py'), may hold values from 0 to 4607, as said below
- elem_count: int32 [4, 8], P('px', 'py'), may hold values from 16 to 64, as said below
Outputs:
- face_values: float32 [4, 8, 4608, 256], P('px', 'py')
- interior_values: bfloat16 [4, 8, 64, 125, 256], P('px', 'py')
Inputs may be any that keep to these rules, and one draw needn't show every extreme that they name: `elem_dof`: rows below 4608 are the partition's own boundary rows; row 4608 + k * 348 + s is the s-th row that the partition shares with its neighbour in direction k. The modes of slot e name only rows r with r % 8 equal to e // 8. Every local row is named by at least two of the partition's modes. `reader_rows`: entry [k, s] is the owned row that the neighbour in direction k refers to by its row 4608 + opp(k) * 348 + s; the 1392 entries of one partition are distinct. `elem_count`: slots at or past a partition's count are empty.
All inputs are finite; a program needn't handle non-finite values.
Results may differ from a plain program's by a relative error of at most 0.0056.
Values may be sent and summed in bfloat16 or wider, within the bound.
A program may use at most 128 MiB of HBM per device.

v0:
```python
import functools

import jax
import jax.numpy as jnp
from jax import lax
from jax.experimental import pallas as pl
from jax.experimental.pallas import tpu as pltpu
from jax.sharding import PartitionSpec as P

GS = 8
LANES = 128
VMEM_BYTES = 58 * 2**20
OPPOSITE = (1, 0, 3, 2)


def round_up(value, unit):
    return (value + unit - 1) // unit * unit


def condense_kernel(
    sizes,
    count_ref,
    readers_ref,
    inverse_ref,
    load_ref,
    coupling_ref,
    weight_ref,
    dof_ref,
    edge_ref,
    owner_ref,
    spread_ref,
    pre_ref,
    pre_weight_ref,
    mine_ref,
    mine_weight_ref,
    picked_ref,
    picked_weight_ref,
    pay_ref,
    pay_weight_ref,
    local_ref,
    local_weight_ref,
    solved_ref,
    coupling_ext_ref,
):
    slots, modes, inner, columns, owned, shared, windows, pad_shared = sizes
    group = pl.program_id(0)
    halves = columns // LANES

    @pl.when(group == 0)
    def _():
        solved_ref[...] = jnp.zeros_like(solved_ref)
        coupling_ext_ref[...] = jnp.zeros_like(coupling_ext_ref)
        picked_ref[...] = jnp.zeros_like(picked_ref)
        picked_weight_ref[...] = jnp.ones_like(picked_weight_ref)
        mine_ref[...] = jnp.zeros_like(mine_ref)
        mine_weight_ref[...] = jnp.ones_like(mine_weight_ref)

    count = count_ref[0, 0]
    lane = lax.broadcasted_iota(jnp.int32, (modes, LANES), 1)
    window_ids = lax.broadcasted_iota(jnp.int32, (windows, modes), 0)
    weight_cols = weight_ref[...].T
    window_of = dof_ref[...] // GS
    weight_total = jnp.zeros((windows, LANES), jnp.float32)
    for e in range(GS):
        live = group * GS + e < count
        solved = jnp.dot(inverse_ref[e], load_ref[e], preferred_element_type=jnp.float32)
        solved = jnp.where(live, solved, 0.0).astype(jnp.bfloat16)
        solved_ref[e, :inner, :] = solved
        coupling_ext_ref[:modes, :inner] = coupling_ref[e]
        col = jnp.where(live, weight_cols[:, e : e + 1], 0.0)
        high = col.astype(jnp.bfloat16).astype(jnp.float32)
        mid = (col - high).astype(jnp.bfloat16).astype(jnp.float32)
        low = col - high - mid
        extra = jnp.where(lane == inner, high, jnp.where(lane == inner + 1, mid, low))
        ext = jnp.where(
            lane < inner, coupling_ext_ref[:modes, :].astype(jnp.float32), extra
        ).astype(jnp.bfloat16)
        onehot = (window_ids == window_of[e : e + 1, :]).astype(jnp.bfloat16)
        spread = jnp.dot(onehot, ext, preferred_element_type=jnp.float32)
        weight_total = weight_total + spread
        spread_ref[:, e * LANES : (e + 1) * LANES] = spread.astype(jnp.bfloat16)

    rows = jnp.dot(
        spread_ref[...],
        solved_ref[...].reshape(GS * LANES, columns),
        preferred_element_type=jnp.float32,
    )
    wide_lane = lax.broadcasted_iota(jnp.int32, (windows, LANES), 1)
    weight_sum = jnp.sum(jnp.where(wide_lane >= inner, weight_total, 0.0), axis=1, keepdims=True)
    for c in range(halves):
        local_ref[c, pl.ds(group, windows, stride=GS), :] = rows[:, c * LANES : (c + 1) * LANES]
    local_weight_ref[pl.ds(group, windows, stride=GS), :] = jnp.broadcast_to(
        weight_sum, (windows, LANES)
    )

    @pl.when(group == pl.num_programs(0) - 1)
    def _():
        def subtract(chunk, carry):
            at = pl.ds(pl.multiple_of(chunk * LANES, LANES), LANES)
            for c in range(halves):
                pre_ref[c, at, :] = (
                    edge_ref[at, c * LANES : (c + 1) * LANES].astype(jnp.float32)
                    - local_ref[c, at, :]
                )
            own = jnp.broadcast_to(owner_ref[pl.ds(chunk, 1), :], (LANES, LANES)).T
            pre_weight_ref[at, :] = own + local_weight_ref[at, :]
            return carry

        lax.fori_loop(0, owned // LANES, subtract, 0)

        def pick(s, carry):
            loaded = []
            for k in range(4):
                r = readers_ref[k, s]
                loaded.append(
                    (
                        [pre_ref[c, pl.ds(r, 1), :] for c in range(halves)],
                        pre_weight_ref[pl.ds(r, 1), :],
                    )
                )
            for k in range(4):
                values, weight = loaded[k]
                for c in range(halves):
                    picked_ref[k, c, pl.ds(s, 1), :] = values[c]
                picked_weight_ref[k, pl.ds(s, 1), :] = weight
            return carry

        lax.fori_loop(0, shared, pick, 0, unroll=4)
        for k in range(4):
            start = owned + k * shared
            for c in range(halves):
                cols = slice(c * LANES, (c + 1) * LANES)
                mine = local_ref[c, start : start + shared, :]
                mine_ref[k, c, :shared, :] = mine
                pay_ref[k, 0, :, cols] = mine_ref[k, c].astype(jnp.bfloat16)
                pay_ref[k, 1, :, cols] = picked_ref[k, c].astype(jnp.bfloat16)
            mine_weight_ref[k, :shared, :] = local_weight_ref[start : start + shared, :]
            sub = lax.broadcasted_iota(jnp.int32, (8, pad_shared), 0)
            pay_weight_ref[k] = jnp.where(
                sub == 0, mine_weight_ref[k].T[:8], picked_weight_ref[k].T[:8]
            )


def exchange_kernel(counts, pay_ref, weight_ref, got_ref, got_weight_ref, send_sem, recv_sem):
    nx, ny = counts
    a, b = lax.axis_index("px"), lax.axis_index("py")
    targets = (
        (lax.rem(a + nx - 1, nx), b),
        (lax.rem(a + 1, nx), b),
        (a, lax.rem(b + ny - 1, ny)),
        (a, lax.rem(b + 1, ny)),
    )
    barrier = pltpu.get_barrier_semaphore()
    for target in targets:
        pl.semaphore_signal(
            barrier, inc=1, device_id=target, device_id_type=pl.DeviceIdType.MESH
        )
    pl.semaphore_wait(barrier, 4)
    copies = []
    for k in range(4):
        for part, (source, dest) in enumerate(((pay_ref, got_ref), (weight_ref, got_weight_ref))):
            copy = pltpu.make_async_remote_copy(
                src_ref=source.at[k],
                dst_ref=dest.at[OPPOSITE[k]],
                send_sem=send_sem.at[part, k],
                recv_sem=recv_sem.at[part, OPPOSITE[k]],
                device_id=targets[k],
                device_id_type=pl.DeviceIdType.MESH,
            )
            copy.start()
            copies.append(copy)
    for copy in copies:
        copy.wait()


def recover_kernel(
    sizes,
    count_ref,
    readers_ref,
    got_ref,
    got_weight_ref,
    pre_ref,
    pre_weight_ref,
    mine_ref,
    mine_weight_ref,
    picked_ref,
    picked_weight_ref,
    spread_ref,
    inverse_ref,
    load_ref,
    face_ref,
    out_ref,
    values_ref,
    ready_ref,
):
    slots, modes, inner, columns, owned, shared, windows, pad_shared = sizes
    group = pl.program_id(0)
    halves = columns // LANES
    groups = slots // GS
    part = owned // groups

    @pl.when(group == 0)
    def _():
        def divide(chunk, carry):
            at = pl.ds(pl.multiple_of(chunk * LANES, LANES), LANES)
            scale = 1.0 / pre_weight_ref[at, :]
            for c in range(halves):
                values_ref[c, at, :] = pre_ref[c, at, :] * scale
            return carry

        lax.fori_loop(0, owned // LANES, divide, 0)
        tail = owned + 4 * shared
        for k in range(4):
            weights = got_weight_ref[k].T
            to_mine = 1.0 / (picked_weight_ref[k] + weights[:, 0:1])
            to_theirs = 1.0 / (mine_weight_ref[k] + weights[:, 1:2])
            start = owned + k * shared
            for c in range(halves):
                cols = slice(c * LANES, (c + 1) * LANES)
                ready_ref[k, c] = (
                    picked_ref[k, c] - got_ref[k, 0, :, cols].astype(jnp.float32)
                ) * to_mine
                theirs = (
                    got_ref[k, 1, :, cols].astype(jnp.float32) - mine_ref[k, c]
                ) * to_theirs
                values_ref[c, start : start + shared, :] = theirs[:shared]
        if windows * GS > tail:
            for c in range(halves):
                values_ref[c, tail:, :] = jnp.zeros((windows * GS - tail, LANES), jnp.float32)

        def place(s, carry):
            loaded = []
            for k in range(4):
                loaded.append([ready_ref[k, c, pl.ds(s, 1), :] for c in range(halves)])
            for k in range(4):
                r = readers_ref[k, s]
                for c in range(halves):
                    values_ref[c, pl.ds(r, 1), :] = loaded[k][c]
            return carry

        lax.fori_loop(0, shared, place, 0, unroll=4)

    at = pl.ds(pl.multiple_of(group * part, 8), part)
    for c in range(halves):
        face_ref[:, c * LANES : (c + 1) * LANES] = values_ref[c, at, :]

    table = jnp.concatenate(
        [values_ref[c, pl.ds(group, windows, stride=GS), :] for c in range(halves)], axis=1
    )
    turned = table.T.astype(jnp.bfloat16)
    pulled_turned = jnp.dot(turned, spread_ref[...], preferred_element_type=jnp.float32)
    count = count_ref[0, 0]
    for e in range(GS):
        live = group * GS + e < count
        pulled = pulled_turned[:, e * LANES : (e + 1) * LANES].T[:inner]
        reduced = (load_ref[e].astype(jnp.float32) - pulled).astype(jnp.bfloat16)
        result = jnp.dot(inverse_ref[e], reduced, preferred_element_type=jnp.float32)
        out_ref[e] = jnp.where(live, result, 0.0).astype(jnp.bfloat16)


def per_device(
    counts,
    coupling,
    interior_inverse,
    interior_load,
    boundary_load,
    owner_weight,
    elem_weight,
    elem_dof,
    reader_rows,
    elem_count,
):
    slots, modes, inner = coupling.shape[2:]
    columns = interior_load.shape[-1]
    owned = boundary_load.shape[2]
    shared = reader_rows.shape[3]
    groups = slots // GS
    halves = columns // LANES
    windows = round_up((owned + 4 * shared) // GS, 16)
    pad_shared = round_up(shared, LANES)
    sizes = (slots, modes, inner, columns, owned, shared, windows, pad_shared)
    f32, bf16 = jnp.float32, jnp.bfloat16
    smem = pl.BlockSpec(memory_space=pltpu.SMEM)
    vmem = pl.BlockSpec(memory_space=pltpu.VMEM)
    anyplace = pl.BlockSpec(memory_space=pl.ANY)

    def by_group(*tail):
        zeros = (0,) * (len(tail))
        return pl.BlockSpec((None, None, GS) + tail, lambda g: (0, 0, g) + zeros)

    spread_spec = pl.BlockSpec((None, windows, GS * LANES), lambda g: (g, 0, 0))
    readers = reader_rows[0, 0]
    params = dict(vmem_limit_bytes=VMEM_BYTES, dimension_semantics=("arbitrary",))
    shape = jax.ShapeDtypeStruct
    (
        spread,
        pre,
        pre_weight,
        mine,
        mine_weight,
        picked,
        picked_weight,
        pay,
        pay_weight,
    ) = pl.pallas_call(
        functools.partial(condense_kernel, sizes),
        grid=(groups,),
        in_specs=[
            smem,
            smem,
            by_group(inner, inner),
            by_group(inner, columns),
            by_group(modes, inner),
            by_group(modes),
            by_group(modes),
            vmem,
            vmem,
        ],
        out_specs=[spread_spec] + [vmem] * 8,
        out_shape=[
            shape((groups, windows, GS * LANES), bf16),
            shape((halves, owned, LANES), f32),
            shape((owned, LANES), f32),
            shape((4, halves, pad_shared, LANES), f32),
            shape((4, pad_shared, LANES), f32),
            shape((4, halves, pad_shared, LANES), f32),
            shape((4, pad_shared, LANES), f32),
            shape((4, 2, pad_shared, columns), bf16),
            shape((4, 8, pad_shared), f32),
        ],
        scratch_shapes=[
            pltpu.VMEM((halves, windows * GS, LANES), f32),
            pltpu.VMEM((windows * GS, LANES), f32),
            pltpu.VMEM((GS, LANES, columns), bf16),
            pltpu.VMEM((round_up(modes, 16), LANES), bf16),
        ],
        compiler_params=pltpu.CompilerParams(**params),
        name="condense",
    )(
        elem_count,
        readers,
        interior_inverse,
        interior_load,
        coupling,
        elem_weight,
        elem_dof,
        boundary_load[0, 0],
        owner_weight.reshape(owned // LANES, LANES),
    )
    got, got_weight = pl.pallas_call(
        functools.partial(exchange_kernel, counts),
        in_specs=[anyplace, anyplace],
        out_specs=[anyplace, anyplace],
        out_shape=[shape(pay.shape, bf16), shape(pay_weight.shape, f32)],
        scratch_shapes=[pltpu.SemaphoreType.DMA((2, 4)), pltpu.SemaphoreType.DMA((2, 4))],
        compiler_params=pltpu.CompilerParams(collective_id=0, has_side_effects=True),
        name="exchange",
    )(pay, pay_weight)
    face, interior = pl.pallas_call(
        functools.partial(recover_kernel, sizes),
        grid=(groups,),
        in_specs=[smem, smem]
        + [vmem] * 8
        + [spread_spec, by_group(inner, inner), by_group(inner, columns)],
        out_specs=[
            pl.BlockSpec((None, None, owned // groups, columns), lambda g: (0, 0, g, 0)),
            by_group(inner, columns),
        ],
        out_shape=[
            shape((1, 1, owned, columns), f32),
            shape((1, 1, slots, inner, columns), bf16),
        ],
        scratch_shapes=[
            pltpu.VMEM((halves, windows * GS, LANES), f32),
            pltpu.VMEM((4, halves, pad_shared, LANES), f32),
        ],
        compiler_params=pltpu.CompilerParams(**params),
        name="recover",
    )(
        elem_count,
        readers,
        got,
        got_weight,
        pre,
        pre_weight,
        mine,
        mine_weight,
        picked,
        picked_weight,
        spread,
        interior_inverse,
        interior_load,
    )
    return face, interior


def solution(mesh):
    in_specs = (
        P("px", "py", None, None, None),
        P("px", "py", None, None, None),
        P("px", "py", None, None, None),
        P("px", "py", None, None),
        P("px", "py", None),
        P("px", "py", None, None),
        P("px", "py", None, None),
        P("px", "py", None, None),
        P("px", "py"),
    )
    out_specs = (P("px", "py", None, None), P("px", "py", None, None, None))
    counts = (mesh.shape["px"], mesh.shape["py"])
    return jax.shard_map(
        functools.partial(per_device, counts),
        mesh=mesh,
        in_specs=in_specs,
        out_specs=out_specs,
        check_vma=False,
    )
```

profile of v0, /device:TPU:0, one launch (start us, length us, event | category | flops | bytes accessed | tf_op | source)
XLA Modules:
  0.0 104.1 jit_solution(3697859096405213693)
XLA Ops:
  1.3 1.4 %reduce = f32[4608]{0:T(1024)} reduce(f32[1,1,4608]{2,1,0:T(1,128)} %param.13, f32[]{:T(128)} %constant.9), dimensions={0,1}, to_apply=%param.13.reduce_sub_computation | reduce | bytes 36868 | tf_op args[4]
  2.6 0.0 copy-start.1
  2.6 4.4 %copy.11.inverse_ref = bf16[1,1,64,125,125]{4,3,2,1,0:T(8,128)(2,1)} copy(bf16[1,1,64,125,125]{4,2,3,1,0:T(8,128)(2,1)} %param.10) | data formatting | bytes 4000000 | tf_op args[1]
  7.1 0.0 copy-done.1
  7.1 0.0 copy-start
  7.1 4.1 %copy.13.coupling_ref = bf16[1,1,64,218,125]{4,3,2,1,0:T(8,128)(2,1)} copy(bf16[1,1,64,218,125]{4,2,3,1,0:T(8,128)(2,1)S(1)} %copy-done.1) | data formatting | bytes 6976000 | tf_op args[0]
  11.2 0.0 copy-done
  11.2 4.3 %copy.12.load_ref = bf16[1,1,64,125,256]{4,3,2,1,0:T(8,128)(2,1)} copy(bf16[1,1,64,125,256]{4,2,3,1,0:T(8,128)(2,1)S(1)} %copy-done) | data formatting | bytes 8192000 | tf_op args[2]
  15.5 34.8 %condense.1 = (bf16[8,752,1024]{2,1,0:T(8,128)(2,1)}, f32[2,4608,128]{2,1,0:T(8,128)}, f32[4608,128]{1,0:T(8,128)}, f32[4,2,384,128]{3,2,1,0:T(8,128)}, f32[4,38...) custom-call(s32[1,1]{1,0:T(1,128)S(6)} %copy.17.count_ref, ...), custom_call_target="tpu_custom_call" | custom-call | tf_op jit(solution)/shard_map/condense/pallas_call | solution.py:305
  50.3 25.4 %exchange.1 = (bf16[4,2,384,256]{3,2,1,0:T(8,128)(2,1)}, f32[4,8,384]{2,1,0:T(8,128)}) custom-call(bf16[4,2,384,256]{3,2,1,0:T(8,128)(2,1)} %get-tuple-element.13.pay_ref, f32[4,8,384]{2,1,0:T(8,128)} %get-tuple-element.14.weight_ref), custom_call_target="tpu_custom_call" | custom-call | tf_op jit(solution)/shard_map/exchange/pallas_call | solution.py:350
  75.7 21.9 %recover.1 = (f32[1,1,4608,256]{3,2,1,0:T(8,128)}, bf16[1,1,64,125,256]{4,3,2,1,0:T(8,128)(2,1)}) custom-call(s32[1,1]{1,0:T(1,128)S(6)} %copy.17.count_ref, s32[4,348]{1,0:T(4,128)} %bitcast.6, bf16[4,2,384,256]{3,2,1,0:T(8,128)(2,1)} %get-tuple-element.15.got_ref, f32[4,8,384]{2,1,0:T(8,128)} %get-tuple-element.16.got_weight_ref, ...), custom_call_target="tpu_custom_call" | custom-call | tf_op jit(solution)/shard_map/recover/pallas_call | solution.py:359
  97.6 6.5 %copy.16 = bf16[1,1,64,125,256]{4,2,3,1,0:T(8,128)(2,1)} copy(bf16[1,1,64,125,256]{4,3,2,1,0:T(8,128)(2,1)} %get-tuple-element.25) | data formatting | bytes 8192000 | tf_op jit(solution)/shard_map/recover/pallas_call | solution.py:359
Async XLA Ops:
  2.6 4.4 %copy-start.1 = (bf16[1,1,64,218,125]{4,2,3,1,0:T(8,128)(2,1)S(1)}, bf16[1,1,64,218,125]{4,2,3,1,0:T(8,128)(2,1)}, u32[]{:S(2)}) copy-start(bf16[1,1,64,218,125]{4,2,3,1,0:T(8,128)(2,1)} %param.9) | copy-start | bytes 10464004
  7.1 4.1 %copy-start = (bf16[1,1,64,125,256]{4,2,3,1,0:T(8,128)(2,1)S(1)}, bf16[1,1,64,125,256]{4,2,3,1,0:T(8,128)(2,1)}, u32[]{:S(2)}) copy-start(bf16[1,1,64,125,256]{4,2,3,1,0:T(8,128)(2,1)} %param.11) | copy-start | bytes 12288004
where the time goes:
time: 104 us
  Pallas kernels  82 us (79%)
  local copies, waits for them, and re-layouts  19.4 us (19%)
  other arithmetic  1.37 us (1%)
  between operations  1.29 us (1%)
    pallas_call x1, Pallas kernels, per_device(): pl.pallas_call(functools.partial(condense_kernel, sizes), grid=(groups,),...  34.8 us
    pallas_call x1, Pallas kernels, per_device(): pl.pallas_call(functools.partial(exchange_kernel, counts), in_specs=[anyp...  25.4 us
    pallas_call x1, Pallas kernels, per_device(): pl.pallas_call(functools.partial(recover_kernel, sizes), grid=(groups,),...  21.9 us
    unnamed x7, local copies, waits for them, and re-layouts  12.9 us
    pallas_call x1, local copies, waits for them, and re-layouts, per_device(): pl.pallas_call(functools.partial(recover_kernel, sizes), grid=(groups,),...  6.5 us

commit v1 on v0

v1 whole, which is shorter than its diff:
```python
import functools

import jax
import jax.numpy as jnp
from jax import lax
from jax.experimental import pallas as pl
from jax.experimental.pallas import tpu as pltpu
from jax.sharding import PartitionSpec as P

GS = 8
LANES = 128
VMEM_BYTES = 58 * 2**20
OPPOSITE = (1, 0, 3, 2)


def round_up(value, unit):
    return (value + unit - 1) // unit * unit


def condense_kernel(
    sizes,
    counts,
    count_ref,
    readers_ref,
    inverse_ref,
    load_ref,
    coupling_ref,
    weight_ref,
    dof_ref,
    edge_ref,
    owner_ref,
    spread_ref,
    inverse_out_ref,
    load_out_ref,
    values_ref,
    ready_ref,
    local_ref,
    local_weight_ref,
    pre_weight_ref,
    solved_ref,
    inverse_rows_ref,
    load_rows_ref,
    coupling_rows_ref,
    picked_ref,
    picked_weight_ref,
    incoming_ref,
    term_pay_ref,
    term_got_ref,
    pick_pay_ref,
    pick_got_ref,
    weight_pay_ref,
    weight_got_ref,
    term_send,
    term_recv,
    last_send,
    last_recv,
):
    slots, modes, inner, columns, owned, shared, windows, pad, span = sizes
    groups = slots // GS
    own_windows = owned // GS
    starts = [min(k * shared // GS, windows - own_windows - span) for k in range(4)]
    shifts = [k * shared - GS * starts[k] for k in range(4)]
    group = pl.program_id(0)
    halves = columns // LANES
    nx, ny = counts
    a, b = lax.axis_index("px"), lax.axis_index("py")
    targets = (
        (lax.rem(a + nx - 1, nx), b),
        (lax.rem(a + 1, nx), b),
        (a, lax.rem(b + ny - 1, ny)),
        (a, lax.rem(b + 1, ny)),
    )

    @pl.when(group == 0)
    def _():
        barrier = pltpu.get_barrier_semaphore()
        for target in targets:
            pl.semaphore_signal(
                barrier, inc=1, device_id=target, device_id_type=pl.DeviceIdType.MESH
            )
        solved_ref[...] = jnp.zeros_like(solved_ref)
        picked_ref[...] = jnp.zeros_like(picked_ref)
        picked_weight_ref[...] = jnp.ones_like(picked_weight_ref)
        pl.semaphore_wait(barrier, 4)

    def remote(source, dest, send_sem, recv_sem, k):
        return pltpu.make_async_remote_copy(
            src_ref=source,
            dst_ref=dest,
            send_sem=send_sem,
            recv_sem=recv_sem,
            device_id=targets[k],
            device_id_type=pl.DeviceIdType.MESH,
        )

    def term_copy(k, g):
        o = OPPOSITE[k]
        return remote(
            term_pay_ref.at[k, g], term_got_ref.at[o, g], term_send.at[k, g], term_recv.at[o, g], k
        )

    def pick_copy(k):
        o = OPPOSITE[k]
        return remote(
            pick_pay_ref.at[k], pick_got_ref.at[o], last_send.at[0, k], last_recv.at[0, o], k
        )

    def weight_copy(k):
        o = OPPOSITE[k]
        return remote(
            weight_pay_ref.at[k], weight_got_ref.at[o], last_send.at[1, k], last_recv.at[1, o], k
        )

    count = count_ref[0, 0]
    lane = lax.broadcasted_iota(jnp.int32, (modes, LANES), 1)
    window_ids = lax.broadcasted_iota(jnp.int32, (windows, modes), 0)
    weight_cols = weight_ref[...].T
    window_of = dof_ref[...] // GS
    inverse_rows_ref[:, :inner] = inverse_ref[...].astype(jnp.float32).reshape(inner * GS, inner)
    coupling_rows_ref[:, :inner] = (
        coupling_ref[...].astype(jnp.float32).reshape(modes * GS, inner)
    )
    load_rows = load_ref[...].astype(jnp.float32).reshape(inner * GS, columns)
    for c in range(halves):
        load_rows_ref[c] = load_rows[:, c * LANES : (c + 1) * LANES]
    weight_total = jnp.zeros((windows, LANES), jnp.float32)
    for e in range(GS):
        live = group * GS + e < count
        inverse = inverse_rows_ref[pl.ds(e, inner, stride=GS), :][:, :inner].astype(jnp.bfloat16)
        load = jnp.concatenate(
            [load_rows_ref[c, pl.ds(e, inner, stride=GS), :] for c in range(halves)], axis=1
        ).astype(jnp.bfloat16)
        inverse_out_ref[e] = inverse
        load_out_ref[e] = load
        solved = jnp.dot(inverse, load, preferred_element_type=jnp.float32)
        solved = jnp.where(live, solved, 0.0).astype(jnp.bfloat16)
        solved_ref[e, :inner, :] = solved
        col = jnp.where(live, weight_cols[:, e : e + 1], 0.0)
        high = col.astype(jnp.bfloat16).astype(jnp.float32)
        mid = (col - high).astype(jnp.bfloat16).astype(jnp.float32)
        low = col - high - mid
        extra = jnp.where(lane == inner, high, jnp.where(lane == inner + 1, mid, low))
        ext = jnp.where(
            lane < inner, coupling_rows_ref[pl.ds(e, modes, stride=GS), :], extra
        ).astype(jnp.bfloat16)
        onehot = (window_ids == window_of[e : e + 1, :]).astype(jnp.bfloat16)
        spread = jnp.dot(onehot, ext, preferred_element_type=jnp.float32)
        weight_total = weight_total + spread
        spread_ref[:, e * LANES : (e + 1) * LANES] = spread.astype(jnp.bfloat16)

    rows = jnp.dot(
        spread_ref[...],
        solved_ref[...].reshape(GS * LANES, columns),
        preferred_element_type=jnp.float32,
    )
    for k in range(4):
        at = own_windows + starts[k]
        term_pay_ref[k, group] = rows[at : at + span].astype(jnp.bfloat16)
        term_copy(k, group).start()
    wide_lane = lax.broadcasted_iota(jnp.int32, (windows, LANES), 1)
    weight_sum = jnp.sum(jnp.where(wide_lane >= inner, weight_total, 0.0), axis=1, keepdims=True)
    for c in range(halves):
        local_ref[c, pl.ds(group, windows, stride=GS), :] = rows[:, c * LANES : (c + 1) * LANES]
    local_weight_ref[pl.ds(group, windows, stride=GS), :] = jnp.broadcast_to(
        weight_sum, (windows, LANES)
    )

    @pl.when(group == groups - 1)
    def _():
        def subtract(chunk, carry):
            at = pl.ds(pl.multiple_of(chunk * LANES, LANES), LANES)
            for c in range(halves):
                values_ref[c, at, :] = (
                    edge_ref[at, c * LANES : (c + 1) * LANES].astype(jnp.float32)
                    - local_ref[c, at, :]
                )
            own = jnp.broadcast_to(owner_ref[pl.ds(chunk, 1), :], (LANES, LANES)).T
            pre_weight_ref[at, :] = own + local_weight_ref[at, :]
            return carry

        lax.fori_loop(0, owned // LANES, subtract, 0)

        for pair in ((0, 1), (2, 3)):

            def pick(s, carry):
                loaded = []
                for k in pair:
                    r = readers_ref[k, s]
                    loaded.append(
                        (
                            [values_ref[c, pl.ds(r, 1), :] for c in range(halves)],
                            pre_weight_ref[pl.ds(r, 1), :],
                        )
                    )
                for k, (values, weight) in zip(pair, loaded):
                    for c in range(halves):
                        picked_ref[k, c, pl.ds(s, 1), :] = values[c]
                    picked_weight_ref[k, pl.ds(s, 1), :] = weight
                return carry

            lax.fori_loop(0, shared, pick, 0, unroll=6)
            for k in pair:
                for c in range(halves):
                    pick_pay_ref[k, :, c * LANES : (c + 1) * LANES] = picked_ref[k, c].astype(
                        jnp.bfloat16
                    )
                pick_copy(k).start()
                start = owned + k * shared
                sub = lax.broadcasted_iota(jnp.int32, (8, pad), 0)
                weight_pay_ref[k] = jnp.where(
                    sub == 0,
                    local_weight_ref[start : start + pad, :].T[:8],
                    picked_weight_ref[k].T[:8],
                )
                weight_copy(k).start()

        def divide(chunk, carry):
            at = pl.ds(pl.multiple_of(chunk * LANES, LANES), LANES)
            scale = 1.0 / pre_weight_ref[at, :]
            for c in range(halves):
                values_ref[c, at, :] = values_ref[c, at, :] * scale
            return carry

        lax.fori_loop(0, owned // LANES, divide, 0)
        tail = owned + 4 * shared
        if windows * GS > tail:
            for c in range(halves):
                values_ref[c, tail:, :] = jnp.zeros((windows * GS - tail, LANES), jnp.float32)

        for k in range(4):

            def settle(g, carry):
                term_copy(k, g).wait()
                return carry

            lax.fori_loop(0, groups, settle, 0)
        for k in range(4):
            for g in range(groups):
                piece = term_got_ref[k, g].astype(jnp.float32)
                for c in range(halves):
                    incoming_ref[k, c, pl.ds(g, span, stride=GS), :] = piece[
                        :, c * LANES : (c + 1) * LANES
                    ]
        for k in (2, 3, 0, 1):
            pick_copy(k).wait_send()
            weight_copy(k).wait_send()
        for k in (3, 2, 1, 0):
            pick_copy(k).wait_recv()
            weight_copy(k).wait_recv()
        for k in range(4):
            weights = weight_got_ref[k].T
            start = owned + k * shared
            to_mine = 1.0 / (picked_weight_ref[k] + weights[:, 0:1])
            to_theirs = 1.0 / (local_weight_ref[start : start + pad, :] + weights[:, 1:2])
            shift = shifts[OPPOSITE[k]]
            for c in range(halves):
                cols = slice(c * LANES, (c + 1) * LANES)
                ready_ref[k, c] = (
                    picked_ref[k, c] - incoming_ref[k, c, shift : shift + pad, :]
                ) * to_mine
                theirs = (
                    pick_got_ref[k, :, cols].astype(jnp.float32)
                    - local_ref[c, start : start + pad, :]
                ) * to_theirs
                values_ref[c, start : start + shared, :] = theirs[:shared]


def recover_kernel(
    sizes,
    count_ref,
    readers_ref,
    values_in_ref,
    ready_ref,
    spread_ref,
    inverse_ref,
    load_ref,
    face_ref,
    out_ref,
    values_ref,
    out_rows_ref,
    in_sem,
    face_sem,
):
    slots, modes, inner, columns, owned, shared, windows, pad, span = sizes
    group = pl.program_id(0)
    halves = columns // LANES
    groups = slots // GS

    def face_copy(c):
        return pltpu.make_async_copy(
            values_ref.at[c, pl.ds(0, owned)],
            face_ref.at[0, 0, :, pl.ds(c * LANES, LANES)],
            face_sem.at[c],
        )

    @pl.when(group == 0)
    def _():
        fetch = pltpu.make_async_copy(values_in_ref, values_ref, in_sem)
        fetch.start()
        fetch.wait()

        def place(s, carry):
            loaded = []
            for k in range(4):
                loaded.append([ready_ref[k, c, pl.ds(s, 1), :] for c in range(halves)])
            for k in range(4):
                r = readers_ref[k, s]
                for c in range(halves):
                    values_ref[c, pl.ds(r, 1), :] = loaded[k][c]
            return carry

        lax.fori_loop(0, shared, place, 0, unroll=4)
        for c in range(halves):
            face_copy(c).start()

    table = jnp.concatenate(
        [values_ref[c, pl.ds(group, windows, stride=GS), :] for c in range(halves)], axis=1
    )
    turned = table.T.astype(jnp.bfloat16)
    pulled_turned = jnp.dot(turned, spread_ref[...], preferred_element_type=jnp.float32)
    count = count_ref[0, 0]
    for e in range(GS):
        live = group * GS + e < count
        pulled = pulled_turned[:, e * LANES : (e + 1) * LANES].T[:inner]
        reduced = (load_ref[e].astype(jnp.float32) - pulled).astype(jnp.bfloat16)
        result = jnp.dot(inverse_ref[e], reduced, preferred_element_type=jnp.float32)
        result = jnp.where(live, result, 0.0)
        for c in range(halves):
            out_rows_ref[c, pl.ds(e, inner, stride=GS), :] = result[:, c * LANES : (c + 1) * LANES]
    out_ref[...] = (
        jnp.concatenate([out_rows_ref[c] for c in range(halves)], axis=1)
        .reshape(inner, GS, columns)
        .astype(jnp.bfloat16)
    )

    @pl.when(group == groups - 1)
    def _():
        for c in range(halves):
            face_copy(c).wait()


def per_device(
    counts,
    coupling,
    interior_inverse,
    interior_load,
    boundary_load,
    owner_weight,
    elem_weight,
    elem_dof,
    reader_rows,
    elem_count,
):
    slots, modes, inner = coupling.shape[2:]
    columns = interior_load.shape[-1]
    owned = boundary_load.shape[2]
    shared = reader_rows.shape[3]
    groups = slots // GS
    halves = columns // LANES
    windows = round_up((owned + 4 * shared) // GS, 16)
    pad = round_up(shared, 16)
    span = round_up(shared // GS + 2, 16)
    sizes = (slots, modes, inner, columns, owned, shared, windows, pad, span)
    f32, bf16 = jnp.float32, jnp.bfloat16
    smem = pl.BlockSpec(memory_space=pltpu.SMEM)
    vmem = pl.BlockSpec(memory_space=pltpu.VMEM)
    anyplace = pl.BlockSpec(memory_space=pl.ANY)

    def by_group(*tail):
        zeros = (0,) * len(tail)
        return pl.BlockSpec((None, None, GS) + tail, lambda g: (0, 0, g) + zeros)

    def by_mode(rows, width):
        return pl.BlockSpec((None, None, rows, GS, width), lambda g: (0, 0, 0, g, 0))

    def by_slot(rows, width):
        return pl.BlockSpec((GS, rows, width), lambda g: (g, 0, 0))

    def modes_first(array):
        return jnp.swapaxes(array, 2, 3)

    spread_spec = pl.BlockSpec((None, windows, GS * LANES), lambda g: (g, 0, 0))
    readers = reader_rows[0, 0]
    params = dict(vmem_limit_bytes=VMEM_BYTES, dimension_semantics=("arbitrary",))
    shape = jax.ShapeDtypeStruct
    spread, inverse_rows, load_rows, values, ready = pl.pallas_call(
        functools.partial(condense_kernel, sizes, counts),
        grid=(groups,),
        in_specs=[
            smem,
            smem,
            by_mode(inner, inner),
            by_mode(inner, columns),
            by_mode(modes, inner),
            by_group(modes),
            by_group(modes),
            vmem,
            vmem,
        ],
        out_specs=[spread_spec, by_slot(inner, inner), by_slot(inner, columns), vmem, vmem],
        out_shape=[
            shape((groups, windows, GS * LANES), bf16),
            shape((slots, inner, inner), bf16),
            shape((slots, inner, columns), bf16),
            shape((halves, windows * GS, LANES), f32),
            shape((4, halves, pad, LANES), f32),
        ],
        scratch_shapes=[
            pltpu.VMEM((halves, windows * GS, LANES), f32),
            pltpu.VMEM((windows * GS, LANES), f32),
            pltpu.VMEM((owned, LANES), f32),
            pltpu.VMEM((GS, LANES, columns), bf16),
            pltpu.VMEM((inner * GS, LANES), f32),
            pltpu.VMEM((halves, inner * GS, LANES), f32),
            pltpu.VMEM((modes * GS, LANES), f32),
            pltpu.VMEM((4, halves, pad, LANES), f32),
            pltpu.VMEM((4, pad, LANES), f32),
            pltpu.VMEM((4, halves, span * GS, LANES), f32),
            pltpu.VMEM((4, groups, span, columns), bf16),
            pltpu.VMEM((4, groups, span, columns), bf16),
            pltpu.VMEM((4, pad, columns), bf16),
            pltpu.VMEM((4, pad, columns), bf16),
            pltpu.VMEM((4, 8, pad), f32),
            pltpu.VMEM((4, 8, pad), f32),
            pltpu.SemaphoreType.DMA((4, groups)),
            pltpu.SemaphoreType.DMA((4, groups)),
            pltpu.SemaphoreType.DMA((2, 4)),
            pltpu.SemaphoreType.DMA((2, 4)),
        ],
        compiler_params=pltpu.CompilerParams(
            collective_id=0, has_side_effects=True, **params
        ),
        name="condense",
    )(
        elem_count,
        readers,
        modes_first(interior_inverse),
        modes_first(interior_load),
        modes_first(coupling),
        elem_weight,
        elem_dof,
        boundary_load[0, 0],
        owner_weight.reshape(owned // LANES, LANES),
    )
    face, interior = pl.pallas_call(
        functools.partial(recover_kernel, sizes),
        grid=(groups,),
        in_specs=[
            smem,
            smem,
            anyplace,
            vmem,
            spread_spec,
            by_slot(inner, inner),
            by_slot(inner, columns),
        ],
        out_specs=[anyplace, by_mode(inner, columns)],
        out_shape=[
            shape((1, 1, owned, columns), f32),
            shape((1, 1, inner, slots, columns), bf16),
        ],
        scratch_shapes=[
            pltpu.VMEM((halves, windows * GS, LANES), f32),
            pltpu.VMEM((halves, inner * GS, LANES), f32),
            pltpu.SemaphoreType.DMA,
            pltpu.SemaphoreType.DMA((halves,)),
        ],
        compiler_params=pltpu.CompilerParams(**params),
        name="recover",
    )(elem_count, readers, values, ready, spread, inverse_rows, load_rows)
    return face, modes_first(interior)


def solution(mesh):
    in_specs = (
        P("px", "py", None, None, None),
        P("px", "py", None, None, None),
        P("px", "py", None, None, None),
        P("px", "py", None, None),
        P("px", "py", None),
        P("px", "py", None, None),
        P("px", "py", None, None),
        P("px", "py", None, None),
        P("px", "py"),
    )
    out_specs = (P("px", "py", None, None), P("px", "py", None, None, None))
    counts = (mesh.shape["px"], mesh.shape["py"])
    return jax.shard_map(
        functools.partial(per_device, counts),
        mesh=mesh,
        in_specs=in_specs,
        out_specs=out_specs,
        check_vma=False,
    )
```

time: 104 us -> 74.5 us (0.72)
  local copies, waits for them, and re-layouts: 19.4 us -> 0 us
  Pallas kernels: 82 us -> 71.5 us
    unnamed x7 -> x0, local copies, waits for them, and re-layouts: 12.9 us -> none
    pallas_call x2 -> x1, Pallas kernels: 60.2 us -> 51.5 us  [per_device(): pl.pallas_call(functools.partial(condense_kernel, sizes, counts), grid=(g...]
    pallas_call x1 -> x0, local copies, waits for them, and re-layouts: 6.5 us -> none  [per_device(): pl.pallas_call(functools.partial(recover_kernel, sizes), grid=(groups,),...]
    pallas_call x1, Pallas kernels: 21.9 us -> 20 us  [per_device(): pl.pallas_call(functools.partial(recover_kernel, sizes), grid=(groups,),...]
where the time goes in v1:
time: 74.5 us; the launch traced here: 74.2 us
  Pallas kernels  71.5 us (96%)
  other arithmetic  1.38 us (2%)
  between operations  1.29 us (2%)
    pallas_call x1, Pallas kernels, per_device(): pl.pallas_call(functools.partial(condense_kernel, sizes, counts), grid=(g...  51.5 us
    pallas_call x1, Pallas kernels, per_device(): pl.pallas_call(functools.partial(recover_kernel, sizes), grid=(groups,),...  20 us

profile of v1, /device:TPU:0, one launch (start us, length us, event | category | flops | bytes accessed | tf_op | source)
XLA Modules:
  0.0 74.2 jit_solution(1815024230356308587)
XLA Ops:
  1.3 1.4 %reduce = f32[4608]{0:T(1024)} reduce(f32[1,1,4608]{2,1,0:T(1,128)} %param.13, f32[]{:T(128)} %constant.9), dimensions={0,1}, to_apply=%param.13.reduce_sub_computation | reduce | bytes 36868 | tf_op args[4]
  2.7 51.5 %condense.1 = (bf16[8,752,1024]{2,1,0:T(8,128)(2,1)}, bf16[64,125,125]{2,1,0:T(8,128)(2,1)}, bf16[64,125,256]{2,1,0:T(8,128)(2,1)}, f32[2,6016,128]{2,1,0:T(8,128)}, f32[4,2,352,128]{3,2,1,0:T(8,128)}) custom-call(s32[1,1]{1,0:T(1,128)S(6)} %copy.11.count_ref, s32[4,348]{1,0:T(4,128)} %bitcast.12, bf16[1,1,125,64,125]{4,3,2,1,0:T(8,128)(2,1)} %bitcast.10, ...), custom_call_target="tpu_custom_call" | custom-call | tf_op jit(solution)/shard_map/condense/pallas_call | solution.py:386
  54.1 20.0 %recover.1 = (f32[1,1,4608,256]{3,2,1,0:T(8,128)}, bf16[1,1,125,64,256]{4,3,2,1,0:T(8,128)(2,1)}) custom-call(s32[1,1]{1,0:T(1,128)S(6)} %copy.11.count_ref, s32[4,348]{1,0:T(4,128)} %bitcast.13, f32[2,6016,128]{2,1,0:T(8,128)} %get-tuple-element.9.values_in_ref, f32[4,2,352,128]{3,2,1,0:T(8,128)} %get-tuple-element.10.ready_ref, ...), custom_call_target="tpu_custom_call" | custom-call | tf_op jit(solution)/shard_map/recover/pallas_call | solution.py:445

commit v2 on v1

v2 whole, which is shorter than its diff:
```python
import functools

import jax
import jax.numpy as jnp
from jax import lax
from jax.experimental import pallas as pl
from jax.experimental.pallas import tpu as pltpu
from jax.sharding import PartitionSpec as P

GS = 8
LANES = 128
VMEM_BYTES = 58 * 2**20
OPPOSITE = (1, 0, 3, 2)


def round_up(value, unit):
    return (value + unit - 1) // unit * unit


def condense_kernel(
    sizes,
    counts,
    count_ref,
    readers_ref,
    inverse_ref,
    load_ref,
    coupling_ref,
    weight_ref,
    dof_ref,
    edge_ref,
    owner_ref,
    reader_rows_ref,
    turned_ref,
    inverse_out_ref,
    load_out_ref,
    face_ref,
    part_ref,
    shared_ref,
    values_ref,
    spread_ref,
    local_ref,
    local_weight_ref,
    pre_weight_ref,
    solved_ref,
    inverse_rows_ref,
    load_rows_ref,
    coupling_rows_ref,
    picked_ref,
    picked_weight_ref,
    incoming_ref,
    added_ref,
    reader_lane_ref,
    added_weight_ref,
    theirs_ref,
    term_pay_ref,
    term_got_ref,
    pick_pay_ref,
    pick_got_ref,
    weight_pay_ref,
    weight_got_ref,
    term_send,
    term_recv,
    last_send,
    last_recv,
    face_sem,
):
    slots, modes, inner, columns, owned, shared, windows, pad, lanes, span = sizes
    groups = slots // GS
    own_windows = owned // GS
    starts = [min(k * shared // GS, windows - own_windows - span) for k in range(4)]
    shifts = [k * shared - GS * starts[k] for k in range(4)]
    step = pl.program_id(0)
    group = lax.rem(step, groups)
    halves = columns // LANES
    nx, ny = counts
    a, b = lax.axis_index("px"), lax.axis_index("py")
    targets = (
        (lax.rem(a + nx - 1, nx), b),
        (lax.rem(a + 1, nx), b),
        (a, lax.rem(b + ny - 1, ny)),
        (a, lax.rem(b + 1, ny)),
    )

    @pl.when(step == 0)
    def _():
        barrier = pltpu.get_barrier_semaphore()
        for target in targets:
            pl.semaphore_signal(
                barrier, inc=1, device_id=target, device_id_type=pl.DeviceIdType.MESH
            )
        solved_ref[...] = jnp.zeros_like(solved_ref)
        picked_ref[...] = jnp.zeros_like(picked_ref)
        picked_weight_ref[...] = jnp.ones_like(picked_weight_ref)
        added_ref[...] = jnp.zeros_like(added_ref)
        reader_lane_ref[...] = jnp.full_like(reader_lane_ref, -1)
        for k in range(4):
            reader_lane_ref[:1, k * lanes : k * lanes + shared] = reader_rows_ref[k : k + 1, :]
        pl.semaphore_wait(barrier, 4)

    def remote(source, dest, send_sem, recv_sem, k):
        return pltpu.make_async_remote_copy(
            src_ref=source,
            dst_ref=dest,
            send_sem=send_sem,
            recv_sem=recv_sem,
            device_id=targets[k],
            device_id_type=pl.DeviceIdType.MESH,
        )

    def term_copy(k, g):
        o = OPPOSITE[k]
        return remote(
            term_pay_ref.at[k, g], term_got_ref.at[o, g], term_send.at[k, g], term_recv.at[o, g], k
        )

    def pick_copy(k):
        o = OPPOSITE[k]
        return remote(
            pick_pay_ref.at[k], pick_got_ref.at[o], last_send.at[0, k], last_recv.at[0, o], k
        )

    def weight_copy(part, k):
        o = OPPOSITE[k]
        return remote(
            weight_pay_ref.at[part, k],
            weight_got_ref.at[part, o],
            last_send.at[part + 1, k],
            last_recv.at[part + 1, o],
            k,
        )

    def face_copy(c):
        return pltpu.make_async_copy(
            values_ref.at[c],
            face_ref.at[0, 0, :, pl.ds(c * LANES, LANES)],
            face_sem.at[c],
        )

    @pl.when(step < groups)
    def _():
        count = count_ref[0, 0]
        lane = lax.broadcasted_iota(jnp.int32, (modes, LANES), 1)
        window_ids = lax.broadcasted_iota(jnp.int32, (windows, modes), 0)
        weight_cols = weight_ref[...].T
        window_of = dof_ref[...] // GS
        inverse_rows_ref[:, :inner] = inverse_ref[...].astype(jnp.float32).reshape(inner * GS, inner)
        coupling_rows_ref[:, :inner] = (
            coupling_ref[...].astype(jnp.float32).reshape(modes * GS, inner)
        )
        load_rows = load_ref[...].astype(jnp.float32).reshape(inner * GS, columns)
        for c in range(halves):
            load_rows_ref[c] = load_rows[:, c * LANES : (c + 1) * LANES]
        weight_total = jnp.zeros((windows, LANES), jnp.float32)
        for e in range(GS):
            live = group * GS + e < count
            inverse = inverse_rows_ref[pl.ds(e, inner, stride=GS), :][:, :inner].astype(jnp.bfloat16)
            load = jnp.concatenate(
                [load_rows_ref[c, pl.ds(e, inner, stride=GS), :] for c in range(halves)], axis=1
            ).astype(jnp.bfloat16)
            inverse_out_ref[e] = inverse
            load_out_ref[e] = load
            solved = jnp.dot(inverse, load, preferred_element_type=jnp.float32)
            solved = jnp.where(live, solved, 0.0).astype(jnp.bfloat16)
            solved_ref[e, :inner, :] = solved
            col = jnp.where(live, weight_cols[:, e : e + 1], 0.0)
            high = col.astype(jnp.bfloat16).astype(jnp.float32)
            mid = (col - high).astype(jnp.bfloat16).astype(jnp.float32)
            low = col - high - mid
            extra = jnp.where(lane == inner, high, jnp.where(lane == inner + 1, mid, low))
            ext = jnp.where(
                lane < inner, coupling_rows_ref[pl.ds(e, modes, stride=GS), :], extra
            ).astype(jnp.bfloat16)
            onehot = (window_ids == window_of[e : e + 1, :]).astype(jnp.bfloat16)
            spread = jnp.dot(onehot, ext, preferred_element_type=jnp.float32)
            weight_total = weight_total + spread
            spread_ref[group, :, e * LANES : (e + 1) * LANES] = spread.astype(jnp.bfloat16)

        rows = jnp.dot(
            spread_ref[group],
            solved_ref[...].reshape(GS * LANES, columns),
            preferred_element_type=jnp.float32,
        )
        turned_ref[...] = spread_ref[group, own_windows:, :].T
        for k in range(4):
            at = own_windows + starts[k]
            term_pay_ref[k, group] = rows[at : at + span].astype(jnp.bfloat16)
            term_copy(k, group).start()
        wide_lane = lax.broadcasted_iota(jnp.int32, (windows, LANES), 1)
        weight_sum = jnp.sum(jnp.where(wide_lane >= inner, weight_total, 0.0), axis=1, keepdims=True)
        for c in range(halves):
            local_ref[c, pl.ds(group, windows, stride=GS), :] = rows[:, c * LANES : (c + 1) * LANES]
        local_weight_ref[pl.ds(group, windows, stride=GS), :] = jnp.broadcast_to(
            weight_sum, (windows, LANES)
        )

    @pl.when(step == groups - 1)
    def _():
        for k in range(4):
            start = owned + k * shared
            weight_pay_ref[0, k] = local_weight_ref[start : start + lanes, :].T[:8]
            weight_copy(0, k).start()

        def subtract(chunk, carry):
            at = pl.ds(pl.multiple_of(chunk * LANES, LANES), LANES)
            for c in range(halves):
                values_ref[c, at, :] = (
                    edge_ref[at, c * LANES : (c + 1) * LANES].astype(jnp.float32)
                    - local_ref[c, at, :]
                )
            own = jnp.broadcast_to(owner_ref[:, at], (LANES, LANES)).T
            pre_weight_ref[at, :] = own + local_weight_ref[at, :]
            return carry

        lax.fori_loop(0, owned // LANES, subtract, 0, unroll=4)

        for pair in ((0, 1), (2, 3)):

            def pick(s, carry):
                loaded = []
                for k in pair:
                    r = readers_ref[k, s]
                    loaded.append(
                        (
                            [values_ref[c, pl.ds(r, 1), :] for c in range(halves)],
                            pre_weight_ref[pl.ds(r, 1), :],
                        )
                    )
                for k, (values, weight) in zip(pair, loaded):
                    for c in range(halves):
                        picked_ref[k, c, pl.ds(s, 1), :] = values[c]
                    picked_weight_ref[k, pl.ds(s, 1), :] = weight
                return carry

            lax.fori_loop(0, shared, pick, 0, unroll=6)
            for k in pair:
                for c in range(halves):
                    pick_pay_ref[k, :, c * LANES : (c + 1) * LANES] = picked_ref[k, c].astype(
                        jnp.bfloat16
                    )
                pick_copy(k).start()
                weight_pay_ref[1, k] = picked_weight_ref[k].T[:8]
                weight_copy(1, k).start()

        for k in range(4):

            def settle(g, carry):
                term_copy(k, g).wait()
                return carry

            lax.fori_loop(0, groups, settle, 0)
            weight_copy(0, k).wait()
        for k in range(4):
            for g in range(groups):
                piece = term_got_ref[k, g].astype(jnp.float32)
                for c in range(halves):
                    incoming_ref[k, c, pl.ds(g, span, stride=GS), :] = piece[
                        :, c * LANES : (c + 1) * LANES
                    ]
            shift = shifts[OPPOSITE[k]]
            for c in range(halves):
                added_ref[k * lanes : k * lanes + pad, c * LANES : (c + 1) * LANES] = incoming_ref[
                    k, c, shift : shift + pad, :
                ].astype(jnp.bfloat16)
            added_weight_ref[:1, k * lanes : (k + 1) * lanes] = weight_got_ref[0, k, :1, :]

        row_ids = lax.broadcasted_iota(jnp.int32, (2 * LANES, 4 * lanes), 0)

        def finish(chunk, carry):
            at = pl.ds(pl.multiple_of(chunk * 2 * LANES, 2 * LANES), 2 * LANES)
            hit = row_ids == reader_lane_ref[:1, :] - chunk * 2 * LANES
            added = jnp.dot(
                hit.astype(jnp.bfloat16), added_ref[...], preferred_element_type=jnp.float32
            )
            weight = jnp.sum(
                jnp.where(hit, added_weight_ref[:1, :], 0.0), axis=1, keepdims=True
            )
            scale = 1.0 / (pre_weight_ref[at, :] + weight)
            for c in range(halves):
                values_ref[c, at, :] = (
                    values_ref[c, at, :] - added[:, c * LANES : (c + 1) * LANES]
                ) * scale
            return carry

        lax.fori_loop(0, owned // (2 * LANES), finish, 0)
        for c in range(halves):
            face_copy(c).start()

    @pl.when(step >= groups)
    def _():
        table = jnp.concatenate(
            [values_ref[c, pl.ds(group, own_windows, stride=GS), :] for c in range(halves)], axis=1
        )
        part_ref[...] = jnp.dot(
            table.T.astype(jnp.bfloat16),
            spread_ref[group, :own_windows, :],
            preferred_element_type=jnp.float32,
        ).T

    @pl.when(step == 2 * groups - 1)
    def _():
        for k in range(4):
            pick_copy(k).wait()
            weight_copy(1, k).wait()
        theirs_ref[...] = jnp.zeros_like(theirs_ref)
        for k in range(4):
            weights = weight_got_ref[1, k].T
            start = owned + k * shared
            scale = 1.0 / (local_weight_ref[start : start + pad, :] + weights[:pad, 0:1])
            for c in range(halves):
                theirs = (
                    pick_got_ref[k, :, c * LANES : (c + 1) * LANES].astype(jnp.float32)
                    - local_ref[c, start : start + pad, :]
                ) * scale
                theirs_ref[c, k * shared : (k + 1) * shared, :] = theirs[:shared]
        for g in range(groups):
            for c in range(halves):
                shared_ref[g, :, c * LANES : (c + 1) * LANES] = theirs_ref[
                    c, pl.ds(g, windows - own_windows, stride=GS), :
                ].astype(jnp.bfloat16)
        for c in range(halves):
            face_copy(c).wait()


def recover_kernel(
    sizes,
    count_ref,
    face_in_ref,
    turned_ref,
    shared_ref,
    part_ref,
    inverse_ref,
    load_ref,
    face_ref,
    out_ref,
    out_rows_ref,
    face_sem,
):
    slots, modes, inner, columns, owned, shared, windows, pad, lanes, span = sizes
    group = pl.program_id(0)
    halves = columns // LANES
    groups = slots // GS

    @pl.when(group == 0)
    def _():
        pltpu.make_async_copy(face_in_ref, face_ref, face_sem).start()

    pulled = part_ref[...] + jnp.dot(
        turned_ref[...], shared_ref[group], preferred_element_type=jnp.float32
    )
    count = count_ref[0, 0]
    for e in range(GS):
        live = group * GS + e < count
        reduced = (
            load_ref[e].astype(jnp.float32) - pulled[e * LANES : e * LANES + inner]
        ).astype(jnp.bfloat16)
        result = jnp.dot(inverse_ref[e], reduced, preferred_element_type=jnp.float32)
        result = jnp.where(live, result, 0.0)
        for c in range(halves):
            out_rows_ref[c, pl.ds(e, inner, stride=GS), :] = result[:, c * LANES : (c + 1) * LANES]
    out_ref[...] = (
        jnp.concatenate([out_rows_ref[c] for c in range(halves)], axis=1)
        .reshape(inner, GS, columns)
        .astype(jnp.bfloat16)
    )

    @pl.when(group == groups - 1)
    def _():
        pltpu.make_async_copy(face_in_ref, face_ref, face_sem).wait()


def per_device(
    counts,
    coupling,
    interior_inverse,
    interior_load,
    boundary_load,
    owner_weight,
    elem_weight,
    elem_dof,
    reader_rows,
    elem_count,
):
    slots, modes, inner = coupling.shape[2:]
    columns = interior_load.shape[-1]
    owned = boundary_load.shape[2]
    shared = reader_rows.shape[3]
    groups = slots // GS
    halves = columns // LANES
    windows = round_up((owned + 4 * shared) // GS, 16)
    pad = round_up(shared, 16)
    span = round_up(shared // GS + 2, 16)
    lanes = round_up(shared, LANES)
    own_windows = owned // GS
    shared_windows = windows - own_windows
    sizes = (slots, modes, inner, columns, owned, shared, windows, pad, lanes, span)
    f32, bf16 = jnp.float32, jnp.bfloat16
    smem = pl.BlockSpec(memory_space=pltpu.SMEM)
    vmem = pl.BlockSpec(memory_space=pltpu.VMEM)
    anyplace = pl.BlockSpec(memory_space=pl.ANY)

    def at_first(g):
        return jnp.minimum(g, groups - 1)

    def by_group(*tail):
        zeros = (0,) * len(tail)
        return pl.BlockSpec((None, None, GS) + tail, lambda g: (0, 0, at_first(g)) + zeros)

    def by_mode(rows, width):
        return pl.BlockSpec(
            (None, None, rows, GS, width), lambda g: (0, 0, 0, at_first(g), 0)
        )

    def by_slot(rows, width):
        return pl.BlockSpec((GS, rows, width), lambda g: (at_first(g), 0, 0))

    def modes_first(array):
        return jnp.swapaxes(array, 2, 3)

    turned_spec = pl.BlockSpec(
        (None, GS * LANES, shared_windows), lambda g: (at_first(g), 0, 0)
    )
    part_block = (None, GS * LANES, columns)
    readers = reader_rows[0, 0]
    params = dict(vmem_limit_bytes=VMEM_BYTES, dimension_semantics=("arbitrary",))
    shape = jax.ShapeDtypeStruct
    turned, inverse_rows, load_rows, face_mid, part, shared_values = pl.pallas_call(
        functools.partial(condense_kernel, sizes, counts),
        grid=(2 * groups,),
        in_specs=[
            smem,
            smem,
            by_mode(inner, inner),
            by_mode(inner, columns),
            by_mode(modes, inner),
            by_group(modes),
            by_group(modes),
            vmem,
            vmem,
            vmem,
        ],
        out_specs=[
            turned_spec,
            by_slot(inner, inner),
            by_slot(inner, columns),
            anyplace,
            pl.BlockSpec(part_block, lambda g: (jnp.maximum(g - groups, 0), 0, 0)),
            vmem,
        ],
        out_shape=[
            shape((groups, GS * LANES, shared_windows), bf16),
            shape((slots, inner, inner), bf16),
            shape((slots, inner, columns), bf16),
            shape((1, 1, owned, columns), f32),
            shape((groups, GS * LANES, columns), f32),
            shape((groups, shared_windows, columns), bf16),
        ],
        scratch_shapes=[
            pltpu.VMEM((halves, owned, LANES), f32),
            pltpu.VMEM((groups, windows, GS * LANES), bf16),
            pltpu.VMEM((halves, windows * GS, LANES), f32),
            pltpu.VMEM((windows * GS + LANES, LANES), f32),
            pltpu.VMEM((owned, LANES), f32),
            pltpu.VMEM((GS, LANES, columns), bf16),
            pltpu.VMEM((inner * GS, LANES), f32),
            pltpu.VMEM((halves, inner * GS, LANES), f32),
            pltpu.VMEM((modes * GS, LANES), f32),
            pltpu.VMEM((4, halves, pad, LANES), f32),
            pltpu.VMEM((4, lanes, LANES), f32),
            pltpu.VMEM((4, halves, span * GS, LANES), f32),
            pltpu.VMEM((4 * lanes, columns), bf16),
            pltpu.VMEM((8, 4 * lanes), jnp.int32),
            pltpu.VMEM((8, 4 * lanes), f32),
            pltpu.VMEM((halves, shared_windows * GS, LANES), f32),
            pltpu.VMEM((4, groups, span, columns), bf16),
            pltpu.VMEM((4, groups, span, columns), bf16),
            pltpu.VMEM((4, pad, columns), bf16),
            pltpu.VMEM((4, pad, columns), bf16),
            pltpu.VMEM((2, 4, 8, lanes), f32),
            pltpu.VMEM((2, 4, 8, lanes), f32),
            pltpu.SemaphoreType.DMA((4, groups)),
            pltpu.SemaphoreType.DMA((4, groups)),
            pltpu.SemaphoreType.DMA((3, 4)),
            pltpu.SemaphoreType.DMA((3, 4)),
            pltpu.SemaphoreType.DMA((halves,)),
        ],
        compiler_params=pltpu.CompilerParams(
            collective_id=0, has_side_effects=True, **params
        ),
        name="condense",
    )(
        elem_count,
        readers,
        modes_first(interior_inverse),
        modes_first(interior_load),
        modes_first(coupling),
        elem_weight,
        elem_dof,
        boundary_load[0, 0],
        owner_weight[0],
        readers,
    )
    face, interior = pl.pallas_call(
        functools.partial(recover_kernel, sizes),
        grid=(groups,),
        in_specs=[
            smem,
            anyplace,
            turned_spec,
            vmem,
            pl.BlockSpec(part_block, lambda g: (g, 0, 0)),
            by_slot(inner, inner),
            by_slot(inner, columns),
        ],
        out_specs=[anyplace, by_mode(inner, columns)],
        out_shape=[
            shape((1, 1, owned, columns), f32),
            shape((1, 1, inner, slots, columns), bf16),
        ],
        scratch_shapes=[
            pltpu.VMEM((halves, inner * GS, LANES), f32),
            pltpu.SemaphoreType.DMA,
        ],
        compiler_params=pltpu.CompilerParams(**params),
        name="recover",
    )(elem_count, face_mid, turned, shared_values, part, inverse_rows, load_rows)
    return face, modes_first(interior)


def solution(mesh):
    in_specs = (
        P("px", "py", None, None, None),
        P("px", "py", None, None, None),
        P("px", "py", None, None, None),
        P("px", "py", None, None),
        P("px", "py", None),
        P("px", "py", None, None),
        P("px", "py", None, None),
        P("px", "py", None, None),
        P("px", "py"),
    )
    out_specs = (P("px", "py", None, None), P("px", "py", None, None, None))
    counts = (mesh.shape["px"], mesh.shape["py"])
    return jax.shard_map(
        functools.partial(per_device, counts),
        mesh=mesh,
        in_specs=in_specs,
        out_specs=out_specs,
        check_vma=False,
    )
```

time: 74.5 us -> 207 us (2.78)
  Pallas kernels: 71.5 us -> 205 us
    pallas_call x1, Pallas kernels: 20 us -> 147 us  [per_device(): pl.pallas_call(functools.partial(recover_kernel, sizes), grid=(groups,),...]
    pallas_call x1, Pallas kernels: 51.5 us -> 58.5 us  [per_device(): pl.pallas_call(functools.partial(condense_kernel, sizes, counts), grid=(2...]
where the time goes in v2:
time: 207 us
  Pallas kernels  205 us (99%)
    pallas_call x1, Pallas kernels, per_device(): pl.pallas_call(functools.partial(recover_kernel, sizes), grid=(groups,),...  147 us
    pallas_call x1, Pallas kernels, per_device(): pl.pallas_call(functools.partial(condense_kernel, sizes, counts), grid=(2...  58.5 us

profile of v2, /device:TPU:0, one launch (start us, length us, event | category | flops | bytes accessed | tf_op | source)
XLA Modules:
  0.0 206.8 jit_solution(347097074871116707)
XLA Ops:
  1.3 58.5 %condense.1 = (bf16[8,1024,176]{2,1,0:T(8,128)(2,1)}, bf16[64,125,125]{2,1,0:T(8,128)(2,1)}, bf16[64,125,256]{2,1,0:T(8,128)(2,1)}, f32[1,1,4608,256]{3,2,1,0:T(...) custom-call(s32[1,1]{1,0:T(1,128)S(6)} %copy.11.count_ref, s32[4,348]{1,0:T(4,128)} %bitcast.11, ...), custom_call_target="tpu_custom_call" | custom-call | tf_op jit(solution)/shard_map/condense/pallas_call | solution.py:426
  59.8 147.0 %recover.1 = (f32[1,1,4608,256]{3,2,1,0:T(8,128)}, bf16[1,1,125,64,256]{4,3,2,1,0:T(8,128)(2,1)}) custom-call(s32[1,1]{1,0:T(1,128)S(6)} %copy.11.count_ref, f32[1,1,4608,256]{3,2,1,0:T(8,128)} %get-tuple-element.10.face_in_ref, bf16[8,1024,176]{2,1,0:T(8,128)(2,1)} %get-tuple-element.11.turned_ref, bf16[8,176,256]{2,1,0:T(8,128)(2,1)} %get-tuple-element.12.shared_ref, ...), custom_call_target="tpu_custom_call" | custom-call | tf_op jit(solution)/shard_map/recover/pallas_call | solution.py:502

commit v3 on v2

--- a/solution.py
+++ b/solution.py
@@ -50,7 +50,6 @@
     incoming_ref,
     added_ref,
     reader_lane_ref,
-    added_weight_ref,
     theirs_ref,
     term_pay_ref,
     term_got_ref,
@@ -140,9 +139,10 @@
     def _():
         count = count_ref[0, 0]
         lane = lax.broadcasted_iota(jnp.int32, (modes, LANES), 1)
-        window_ids = lax.broadcasted_iota(jnp.int32, (windows, modes), 0)
+        one, zero = jnp.bfloat16(1), jnp.bfloat16(0)
+        window_ids = lax.broadcasted_iota(jnp.int32, (windows, modes), 0).astype(jnp.int16)
         weight_cols = weight_ref[...].T
-        window_of = dof_ref[...] // GS
+        window_of = (dof_ref[...] // GS).astype(jnp.int16)
         inverse_rows_ref[:, :inner] = inverse_ref[...].astype(jnp.float32).reshape(inner * GS, inner)
         coupling_rows_ref[:, :inner] = (
             coupling_ref[...].astype(jnp.float32).reshape(modes * GS, inner)
@@ -170,7 +170,9 @@
             ext = jnp.where(
                 lane < inner, coupling_rows_ref[pl.ds(e, modes, stride=GS), :], extra
             ).astype(jnp.bfloat16)
-            onehot = (window_ids == window_of[e : e + 1, :]).astype(jnp.bfloat16)
+            onehot = jnp.where(
+                window_ids == window_of[e : e + 1, :], one, zero
+            )
             spread = jnp.dot(onehot, ext, preferred_element_type=jnp.float32)
             weight_total = weight_total + spread
             spread_ref[group, :, e * LANES : (e + 1) * LANES] = spread.astype(jnp.bfloat16)
@@ -257,28 +259,31 @@
                         :, c * LANES : (c + 1) * LANES
                     ]
             shift = shifts[OPPOSITE[k]]
+            before = picked_weight_ref[k, :pad, :]
+            after = 1.0 / (before + weight_got_ref[0, k].T[:pad, 0:1])
+            before = 1.0 / before
+            real = lax.broadcasted_iota(jnp.int32, (pad, LANES), 0) < shared
             for c in range(halves):
-                added_ref[k * lanes : k * lanes + pad, c * LANES : (c + 1) * LANES] = incoming_ref[
-                    k, c, shift : shift + pad, :
-                ].astype(jnp.bfloat16)
-            added_weight_ref[:1, k * lanes : (k + 1) * lanes] = weight_got_ref[0, k, :1, :]
-
-        row_ids = lax.broadcasted_iota(jnp.int32, (2 * LANES, 4 * lanes), 0)
+                picked = picked_ref[k, c]
+                incoming = incoming_ref[k, c, shift : shift + pad, :]
+                change = (picked - incoming) * after - picked * before
+                added_ref[k * lanes : k * lanes + pad, c * LANES : (c + 1) * LANES] = jnp.where(
+                    real, change, 0.0
+                ).astype(jnp.bfloat16)
+
+        row_ids = lax.broadcasted_iota(jnp.int32, (2 * LANES, 4 * lanes), 0).astype(jnp.int16)
+        one, zero = jnp.bfloat16(1), jnp.bfloat16(0)
 
         def finish(chunk, carry):
             at = pl.ds(pl.multiple_of(chunk * 2 * LANES, 2 * LANES), 2 * LANES)
-            hit = row_ids == reader_lane_ref[:1, :] - chunk * 2 * LANES
-            added = jnp.dot(
-                hit.astype(jnp.bfloat16), added_ref[...], preferred_element_type=jnp.float32
-            )
-            weight = jnp.sum(
-                jnp.where(hit, added_weight_ref[:1, :], 0.0), axis=1, keepdims=True
-            )
-            scale = 1.0 / (pre_weight_ref[at, :] + weight)
+            wanted = (reader_lane_ref[:1, :] - chunk * 2 * LANES).astype(jnp.int16)
+            onehot = jnp.where(row_ids == wanted, one, zero)
+            added = jnp.dot(onehot, added_ref[...], preferred_element_type=jnp.float32)
+            scale = 1.0 / pre_weight_ref[at, :]
             for c in range(halves):
                 values_ref[c, at, :] = (
-                    values_ref[c, at, :] - added[:, c * LANES : (c + 1) * LANES]
-                ) * scale
+                    values_ref[c, at, :] * scale + added[:, c * LANES : (c + 1) * LANES]
+                )
             return carry
 
         lax.fori_loop(0, owned // (2 * LANES), finish, 0)
@@ -333,17 +338,13 @@
     face_ref,
     out_ref,
     out_rows_ref,
-    face_sem,
 ):
     slots, modes, inner, columns, owned, shared, windows, pad, lanes, span = sizes
     group = pl.program_id(0)
     halves = columns // LANES
     groups = slots // GS
 
-    @pl.when(group == 0)
-    def _():
-        pltpu.make_async_copy(face_in_ref, face_ref, face_sem).start()
-
+    face_ref[...] = face_in_ref[...]
     pulled = part_ref[...] + jnp.dot(
         turned_ref[...], shared_ref[group], preferred_element_type=jnp.float32
     )
@@ -362,10 +363,6 @@
         .reshape(inner, GS, columns)
         .astype(jnp.bfloat16)
     )
-
-    @pl.when(group == groups - 1)
-    def _():
-        pltpu.make_async_copy(face_in_ref, face_ref, face_sem).wait()
 
 
 def per_device(
@@ -419,6 +416,7 @@
     turned_spec = pl.BlockSpec(
         (None, GS * LANES, shared_windows), lambda g: (at_first(g), 0, 0)
     )
+    face_spec = pl.BlockSpec((None, None, owned // groups, columns), lambda g: (0, 0, g, 0))
     part_block = (None, GS * LANES, columns)
     readers = reader_rows[0, 0]
     params = dict(vmem_limit_bytes=VMEM_BYTES, dimension_semantics=("arbitrary",))
@@ -469,7 +467,6 @@
             pltpu.VMEM((4, halves, span * GS, LANES), f32),
             pltpu.VMEM((4 * lanes, columns), bf16),
             pltpu.VMEM((8, 4 * lanes), jnp.int32),
-            pltpu.VMEM((8, 4 * lanes), f32),
             pltpu.VMEM((halves, shared_windows * GS, LANES), f32),
             pltpu.VMEM((4, groups, span, columns), bf16),
             pltpu.VMEM((4, groups, span, columns), bf16),
@@ -504,21 +501,20 @@
         grid=(groups,),
         in_specs=[
             smem,
-            anyplace,
+            face_spec,
             turned_spec,
             vmem,
             pl.BlockSpec(part_block, lambda g: (g, 0, 0)),
             by_slot(inner, inner),
             by_slot(inner, columns),
         ],
-        out_specs=[anyplace, by_mode(inner, columns)],
+        out_specs=[face_spec, by_mode(inner, columns)],
         out_shape=[
             shape((1, 1, owned, columns), f32),
             shape((1, 1, inner, slots, columns), bf16),
         ],
         scratch_shapes=[
             pltpu.VMEM((halves, inner * GS, LANES), f32),
-            pltpu.SemaphoreType.DMA,
         ],
         compiler_params=pltpu.CompilerParams(**params),
         name="recover",

time: 207 us -> 71.5 us (0.35)
  Pallas kernels: 205 us -> 70 us
    pallas_call x1, Pallas kernels: 147 us -> 14.9 us  [per_device(): pl.pallas_call(functools.partial(recover_kernel, sizes), grid=(groups,),...]
    pallas_call x1, Pallas kernels: 58.5 us -> 55.1 us  [per_device(): pl.pallas_call(functools.partial(condense_kernel, sizes, counts), grid=(2...]
where the time goes in v3:
time: 71.5 us; the launch traced here: 71.2 us
  Pallas kernels  70 us (98%)
  between operations  1.29 us (2%)
    pallas_call x1, Pallas kernels, per_device(): pl.pallas_call(functools.partial(condense_kernel, sizes, counts), grid=(2...  55.1 us
    pallas_call x1, Pallas kernels, per_device(): pl.pallas_call(functools.partial(recover_kernel, sizes), grid=(groups,),...  14.9 us

profile of v3, /device:TPU:0, one launch (start us, length us, event | category | flops | bytes accessed | tf_op | source)
XLA Modules:
  0.0 71.2 jit_solution(568761385681263771)
XLA Ops:
  1.3 55.1 %condense.1 = (bf16[8,1024,176]{2,1,0:T(8,128)(2,1)}, bf16[64,125,125]{2,1,0:T(8,128)(2,1)}, bf16[64,125,256]{2,1,0:T(8,128)(2,1)}, f32[1,1,4608,256]{3,2,1,0:T(...) custom-call(s32[1,1]{1,0:T(1,128)S(6)} %copy.11.count_ref, s32[4,348]{1,0:T(4,128)} %bitcast.11, ...), custom_call_target="tpu_custom_call" | custom-call | tf_op jit(solution)/shard_map/condense/pallas_call | solution.py:424
  56.4 14.9 %recover.1 = (f32[1,1,4608,256]{3,2,1,0:T(8,128)}, bf16[1,1,125,64,256]{4,3,2,1,0:T(8,128)(2,1)}) custom-call(s32[1,1]{1,0:T(1,128)S(6)} %copy.11.count_ref, f32[1,1,4608,256]{3,2,1,0:T(8,128)} %get-tuple-element.10.face_in_ref, bf16[8,1024,176]{2,1,0:T(8,128)(2,1)} %get-tuple-element.11.turned_ref, bf16[8,176,256]{2,1,0:T(8,128)(2,1)} %get-tuple-element.12.shared_ref, ...), custom_call_target="tpu_custom_call" | custom-call | tf_op jit(solution)/shard_map/recover/pallas_call | solution.py:499

commit v4 on v3

--- a/solution.py
+++ b/solution.py
@@ -30,14 +30,13 @@
     edge_ref,
     owner_ref,
     reader_rows_ref,
-    turned_ref,
-    inverse_out_ref,
-    load_out_ref,
     face_ref,
-    part_ref,
-    shared_ref,
+    out_ref,
     values_ref,
     spread_ref,
+    inverse_all_ref,
+    load_all_ref,
+    out_rows_ref,
     local_ref,
     local_weight_ref,
     pre_weight_ref,
@@ -157,8 +156,8 @@
             load = jnp.concatenate(
                 [load_rows_ref[c, pl.ds(e, inner, stride=GS), :] for c in range(halves)], axis=1
             ).astype(jnp.bfloat16)
-            inverse_out_ref[e] = inverse
-            load_out_ref[e] = load
+            inverse_all_ref[group * GS + e] = inverse
+            load_all_ref[group * GS + e] = load
             solved = jnp.dot(inverse, load, preferred_element_type=jnp.float32)
             solved = jnp.where(live, solved, 0.0).astype(jnp.bfloat16)
             solved_ref[e, :inner, :] = solved
@@ -182,7 +181,6 @@
             solved_ref[...].reshape(GS * LANES, columns),
             preferred_element_type=jnp.float32,
         )
-        turned_ref[...] = spread_ref[group, own_windows:, :].T
         for k in range(4):
             at = own_windows + starts[k]
             term_pay_ref[k, group] = rows[at : at + span].astype(jnp.bfloat16)
@@ -290,20 +288,9 @@
         for c in range(halves):
             face_copy(c).start()
 
-    @pl.when(step >= groups)
-    def _():
-        table = jnp.concatenate(
-            [values_ref[c, pl.ds(group, own_windows, stride=GS), :] for c in range(halves)], axis=1
-        )
-        part_ref[...] = jnp.dot(
-            table.T.astype(jnp.bfloat16),
-            spread_ref[group, :own_windows, :],
-            preferred_element_type=jnp.float32,
-        ).T
-
-    @pl.when(step == 2 * groups - 1)
-    def _():
-        for k in range(4):
+    @pl.when(step == groups)
+    def _():
+        for k in (2, 3, 0, 1):
             pick_copy(k).wait()
             weight_copy(1, k).wait()
         theirs_ref[...] = jnp.zeros_like(theirs_ref)
@@ -317,52 +304,47 @@
                     - local_ref[c, start : start + pad, :]
                 ) * scale
                 theirs_ref[c, k * shared : (k + 1) * shared, :] = theirs[:shared]
-        for g in range(groups):
+
+    @pl.when(step >= groups)
+    def _():
+        table = jnp.concatenate(
+            [
+                jnp.concatenate(
+                    [
+                        values_ref[c, pl.ds(group, own_windows, stride=GS), :],
+                        theirs_ref[c, pl.ds(group, windows - own_windows, stride=GS), :],
+                    ],
+                    axis=0,
+                )
+                for c in range(halves)
+            ],
+            axis=1,
+        )
+        pulled = jnp.dot(
+            table.T.astype(jnp.bfloat16), spread_ref[group], preferred_element_type=jnp.float32
+        )
+        for e in range(GS):
+            slot = group * GS + e
+            part = pulled[:, e * LANES : (e + 1) * LANES].T[:inner]
+            reduced = (load_all_ref[slot].astype(jnp.float32) - part).astype(jnp.bfloat16)
+            result = jnp.dot(
+                inverse_all_ref[slot], reduced, preferred_element_type=jnp.float32
+            )
+            result = jnp.where(slot < count_ref[0, 0], result, 0.0)
             for c in range(halves):
-                shared_ref[g, :, c * LANES : (c + 1) * LANES] = theirs_ref[
-                    c, pl.ds(g, windows - own_windows, stride=GS), :
-                ].astype(jnp.bfloat16)
+                out_rows_ref[c, pl.ds(e, inner, stride=GS), :] = result[
+                    :, c * LANES : (c + 1) * LANES
+                ]
+        out_ref[...] = (
+            jnp.concatenate([out_rows_ref[c] for c in range(halves)], axis=1)
+            .reshape(inner, GS, columns)
+            .astype(jnp.bfloat16)
+        )
+
+    @pl.when(step == 2 * groups - 1)
+    def _():
         for c in range(halves):
             face_copy(c).wait()
-
-
-def recover_kernel(
-    sizes,
-    count_ref,
-    face_in_ref,
-    turned_ref,
-    shared_ref,
-    part_ref,
-    inverse_ref,
-    load_ref,
-    face_ref,
-    out_ref,
-    out_rows_ref,
-):
-    slots, modes, inner, columns, owned, shared, windows, pad, lanes, span = sizes
-    group = pl.program_id(0)
-    halves = columns // LANES
-    groups = slots // GS
-
-    face_ref[...] = face_in_ref[...]
-    pulled = part_ref[...] + jnp.dot(
-        turned_ref[...], shared_ref[group], preferred_element_type=jnp.float32
-    )
-    count = count_ref[0, 0]
-    for e in range(GS):
-        live = group * GS + e < count
-        reduced = (
-            load_ref[e].astype(jnp.float32) - pulled[e * LANES : e * LANES + inner]
-        ).astype(jnp.bfloat16)
-        result = jnp.dot(inverse_ref[e], reduced, preferred_element_type=jnp.float32)
-        result = jnp.where(live, result, 0.0)
-        for c in range(halves):
-            out_rows_ref[c, pl.ds(e, inner, stride=GS), :] = result[:, c * LANES : (c + 1) * LANES]
-    out_ref[...] = (
-        jnp.concatenate([out_rows_ref[c] for c in range(halves)], axis=1)
-        .reshape(inner, GS, columns)
-        .astype(jnp.bfloat16)
-    )
 
 
 def per_device(
@@ -407,21 +389,13 @@
             (None, None, rows, GS, width), lambda g: (0, 0, 0, at_first(g), 0)
         )
 
-    def by_slot(rows, width):
-        return pl.BlockSpec((GS, rows, width), lambda g: (at_first(g), 0, 0))
-
     def modes_first(array):
         return jnp.swapaxes(array, 2, 3)
 
-    turned_spec = pl.BlockSpec(
-        (None, GS * LANES, shared_windows), lambda g: (at_first(g), 0, 0)
-    )
-    face_spec = pl.BlockSpec((None, None, owned // groups, columns), lambda g: (0, 0, g, 0))
-    part_block = (None, GS * LANES, columns)
     readers = reader_rows[0, 0]
     params = dict(vmem_limit_bytes=VMEM_BYTES, dimension_semantics=("arbitrary",))
     shape = jax.ShapeDtypeStruct
-    turned, inverse_rows, load_rows, face_mid, part, shared_values = pl.pallas_call(
+    face, interior = pl.pallas_call(
         functools.partial(condense_kernel, sizes, counts),
         grid=(2 * groups,),
         in_specs=[
@@ -437,24 +411,22 @@
             vmem,
         ],
         out_specs=[
-            turned_spec,
-            by_slot(inner, inner),
-            by_slot(inner, columns),
             anyplace,
-            pl.BlockSpec(part_block, lambda g: (jnp.maximum(g - groups, 0), 0, 0)),
-            vmem,
+            pl.BlockSpec(
+                (None, None, inner, GS, columns),
+                lambda g: (0, 0, 0, jnp.maximum(g - groups, 0), 0),
+            ),
         ],
         out_shape=[
-            shape((groups, GS * LANES, shared_windows), bf16),
-            shape((slots, inner, inner), bf16),
-            shape((slots, inner, columns), bf16),
             shape((1, 1, owned, columns), f32),
-            shape((groups, GS * LANES, columns), f32),
-            shape((groups, shared_windows, columns), bf16),
+            shape((1, 1, inner, slots, columns), bf16),
         ],
         scratch_shapes=[
             pltpu.VMEM((halves, owned, LANES), f32),
             pltpu.VMEM((groups, windows, GS * LANES), bf16),
+            pltpu.VMEM((slots, inner, inner), bf16),
+            pltpu.VMEM((slots, inner, columns), bf16),
+            pltpu.VMEM((halves, inner * GS, LANES), f32),
             pltpu.VMEM((halves, windows * GS, LANES), f32),
             pltpu.VMEM((windows * GS + LANES, LANES), f32),
             pltpu.VMEM((owned, LANES), f32),
@@ -483,7 +455,7 @@
         compiler_params=pltpu.CompilerParams(
             collective_id=0, has_side_effects=True, **params
         ),
-        name="condense",
+        name="condense_recover",
     )(
         elem_count,
         readers,
@@ -496,29 +468,6 @@
         owner_weight[0],
         readers,
     )
-    face, interior = pl.pallas_call(
-        functools.partial(recover_kernel, sizes),
-        grid=(groups,),
-        in_specs=[
-            smem,
-            face_spec,
-            turned_spec,
-            vmem,
-            pl.BlockSpec(part_block, lambda g: (g, 0, 0)),
-            by_slot(inner, inner),
-            by_slot(inner, columns),
-        ],
-        out_specs=[face_spec, by_mode(inner, columns)],
-        out_shape=[
-            shape((1, 1, owned, columns), f32),
-            shape((1, 1, inner, slots, columns), bf16),
-        ],
-        scratch_shapes=[
-            pltpu.VMEM((halves, inner * GS, LANES), f32),
-        ],
-        compiler_params=pltpu.CompilerParams(**params),
-        name="recover",
-    )(elem_count, face_mid, turned, shared_values, part, inverse_rows, load_rows)
     return face, modes_first(interior)
 
 

time: 71.5 us -> 63.6 us (0.89)
  Pallas kernels: 70 us -> 55.2 us
  local copies, waits for them, and re-layouts: 0 us -> 6.98 us
    pallas_call x1 -> x0, Pallas kernels: 14.9 us -> none  [per_device(): pl.pallas_call(functools.partial(recover_kernel, sizes), grid=(groups,),...]
    unnamed x0 -> x4, local copies, waits for them, and re-layouts: none -> 6.98 us
where the time goes in v4:
time: 63.6 us; the launch traced here: 63.5 us
  Pallas kernels  55.2 us (87%)
  local copies, waits for them, and re-layouts  6.98 us (11%)
  between operations  1.3 us (2%)
    pallas_call x1, Pallas kernels, per_device(): pl.pallas_call(functools.partial(condense_kernel, sizes, counts), grid=(2...  55.2 us
    unnamed x4, local copies, waits for them, and re-layouts  6.98 us

profile of v4, /device:TPU:0, one launch (start us, length us, event | category | flops | bytes accessed | tf_op | source)
XLA Modules:
  0.0 63.5 jit_solution(2036858502721624236)
XLA Ops:
  1.3 55.2 %condense_recover.1 = (f32[1,1,4608,256]{3,2,1,0:T(8,128)}, bf16[1,1,125,64,256]{4,3,2,1,0:T(8,128)(2,1)}) custom-call(s32[1,1]{1,0:T(1,128)S(6)} %copy.13.count_ref, s32[4,348]{1,0:T(4,128)} %bitcast.12, bf16[1,1,125,64,125]{4,3,2,1,0:T(8,128)(2,1)} %bitcast.11, bf16[1,1,125,64,256]{4,3,2,1,0:T(8,128)(2,1)} %bitcast.8, ...), custom_call_target="tpu_custom_call" | custom-call | tf_op jit(solution)/shard_map/condense_recover/pallas_call | solution.py:398
  56.5 0.0 copy-start
  56.5 5.0 %copy.14 = f32[1,1,4608,256]{3,2,1,0:T(8,128)} copy(f32[1,1,4608,256]{3,2,1,0:T(8,128)} %get-tuple-element.8) | data formatting | bytes 9437184
  61.5 0.0 copy-done
  61.5 2.0 %copy.15 = bf16[1,1,64,125,256]{4,2,3,1,0:T(8,128)(2,1)} copy(bf16[1,1,64,125,256]{4,2,3,1,0:T(8,128)(2,1)S(1)} %bitcast.7) | data formatting | bytes 8192000
Async XLA Ops:
  56.5 5.0 %copy-start = (bf16[1,1,125,64,256]{4,3,2,1,0:T(8,128)(2,1)S(1)}, bf16[1,1,125,64,256]{4,3,2,1,0:T(8,128)(2,1)}, u32[]{:S(2)}) copy-start(bf16[1,1,125,64,256]{4,3,2,1,0:T(8,128)(2,1)} %get-tuple-element.5) | copy-start | bytes 12288004

commit v5 on v4

--- a/solution.py
+++ b/solution.py
@@ -211,7 +211,7 @@
             pre_weight_ref[at, :] = own + local_weight_ref[at, :]
             return carry
 
-        lax.fori_loop(0, owned // LANES, subtract, 0, unroll=4)
+        lax.fori_loop(0, owned // LANES, subtract, 0, unroll=6)
 
         for pair in ((0, 1), (2, 3)):
 
@@ -231,7 +231,7 @@
                     picked_weight_ref[k, pl.ds(s, 1), :] = weight
                 return carry
 
-            lax.fori_loop(0, shared, pick, 0, unroll=6)
+            lax.fori_loop(0, shared, pick, 0, unroll=12)
             for k in pair:
                 for c in range(halves):
                     pick_pay_ref[k, :, c * LANES : (c + 1) * LANES] = picked_ref[k, c].astype(
@@ -284,7 +284,7 @@
                 )
             return carry
 
-        lax.fori_loop(0, owned // (2 * LANES), finish, 0)
+        lax.fori_loop(0, owned // (2 * LANES), finish, 0, unroll=3)
         for c in range(halves):
             face_copy(c).start()
 

time: 63.6 us -> 63.2 us (level)
  no operation moved by 1% of the time
where the time goes in v5:
time: 63.2 us; the launch traced here: 63.1 us
  Pallas kernels  54.8 us (87%)
  local copies, waits for them, and re-layouts  6.98 us (11%)
  between operations  1.3 us (2%)
    pallas_call x1, Pallas kernels, per_device(): pl.pallas_call(functools.partial(condense_kernel, sizes, counts), grid=(2...  54.8 us
    unnamed x4, local copies, waits for them, and re-layouts  6.98 us

profile of v5, /device:TPU:0, one launch (start us, length us, event | category | flops | bytes accessed | tf_op | source)
XLA Modules:
  0.0 63.1 jit_solution(7834749695747458828)
XLA Ops:
  1.3 54.8 %condense_recover.1 = (f32[1,1,4608,256]{3,2,1,0:T(8,128)}, bf16[1,1,125,64,256]{4,3,2,1,0:T(8,128)(2,1)}) custom-call(s32[1,1]{1,0:T(1,128)S(6)} %copy.13.count_ref, s32[4,348]{1,0:T(4,128)} %bitcast.12, bf16[1,1,125,64,125]{4,3,2,1,0:T(8,128)(2,1)} %bitcast.11, bf16[1,1,125,64,256]{4,3,2,1,0:T(8,128)(2,1)} %bitcast.8, ...), custom_call_target="tpu_custom_call" | custom-call | tf_op jit(solution)/shard_map/condense_recover/pallas_call | solution.py:398
  56.1 0.0 copy-start
  56.1 5.0 %copy.14 = f32[1,1,4608,256]{3,2,1,0:T(8,128)} copy(f32[1,1,4608,256]{3,2,1,0:T(8,128)} %get-tuple-element.8) | data formatting | bytes 9437184
  61.1 0.0 copy-done
  61.1 2.0 %copy.15 = bf16[1,1,64,125,256]{4,2,3,1,0:T(8,128)(2,1)} copy(bf16[1,1,64,125,256]{4,2,3,1,0:T(8,128)(2,1)S(1)} %bitcast.7) | data formatting | bytes 8192000
Async XLA Ops:
  56.1 5.0 %copy-start = (bf16[1,1,125,64,256]{4,3,2,1,0:T(8,128)(2,1)S(1)}, bf16[1,1,125,64,256]{4,3,2,1,0:T(8,128)(2,1)}, u32[]{:S(2)}) copy-start(bf16[1,1,125,64,256]{4,3,2,1,0:T(8,128)(2,1)} %get-tuple-element.5) | copy-start | bytes 12288004
